TPU v7x, 32 devices: a whole 2x2x4 slice. The times are simulated.
32 devices in a mesh: dom: 8 (over y, x, core), blk: 4 (over z).
Axes of the slice: x: 2, y: 2, z: 4, core: 2. Of those that a mesh axis runs over, the one named last changes fastest.
Arguments:
- features: bfloat16 [32768, 128], P(('dom', 'blk')), may hold values from -6 to 6
- tile_vals: bfloat16 [2304, 128, 128], P(('dom', 'blk')), may hold values from -0.25 to 0.25
- tile_rows: int32 [32, 72], P(('dom', 'blk')), may hold values from 0 to 7
- tile_cols: int32 [32, 72], P(('dom', 'blk')), may hold values from 0 to 7
- tile_count: int32 [32, 4], P(('dom', 'blk')), may hold values from 1 to 18, as said below
- cut_weights: bfloat16 [32768, 384], P(('dom', 'blk')), may hold values from -0.4375 to 0.4375
- send_idx: int32 [32, 384], P(('dom', 'blk')), may hold values from 0 to 1023
- send_count: int32 [32, 8], P(('dom', 'blk')), may hold values from 0 to 48, as said below
- weight: bfloat16 [128, 256], replicated, may hold values from -0.5 to 0.5
- bias: float32 [256], replicated, may hold values from -3 to 3
- cotangent: bfloat16 [32768, 256], P(('dom', 'blk')), may hold values from -6 to 6
Outputs:
- out_y: bfloat16 [32768, 256], P(('dom', 'blk'))
- grad_x: bfloat16 [32768, 128], P(('dom', 'blk'))
- grad_w: float32 [128, 256], replicated
- grad_b: float32 [256], replicated
Inputs may be any that keep to these rules, and one draw needn't show every extreme that they name: `tile_count`: every device has a source position with exactly 18 live slots; devices differ strongly in their counts. `send_count`: zero toward a device's own group; at each index along blk some group receives exactly 48 rows from every other group.
All inputs are finite; a program needn't handle non-finite values.
Results may differ from a plain program's by a relative error of at most 0.018.
Values may be sent and summed in bfloat16 or wider, within the bound.
A program may use at most 128 MiB of HBM per device.

v0:
```python
import math
import jax
import jax.numpy as jnp
from jax import lax
from jax.sharding import PartitionSpec as P


def pad_piece(piece, tile_side):
    padding = jnp.zeros((tile_side, piece.shape[1]), piece.dtype)
    return jnp.concatenate([padding, piece, padding], axis=0)


def pick_blocks(padded, piece_rows, first_rows, tile_side):
    places = jnp.clip(first_rows + tile_side, 0, piece_rows + tile_side)
    picked = jax.vmap(lambda where_at: lax.dynamic_slice_in_dim(padded, where_at, tile_side, 0))(
        places
    )
    inside = (first_rows > -tile_side) & (first_rows < piece_rows)
    return (picked, inside)


def accumulate(running, tiles_here, picked, target, live, flipped):
    row_blocks = running.shape[0]
    selector = (
        (target[:, None] == jnp.arange(row_blocks, dtype=jnp.int32)[None, :]) & live[:, None]
    ).astype(tiles_here.dtype)
    pattern = "tr,tji,tjf->rif" if flipped else "tr,tij,tjf->rif"
    return running + jnp.einsum(
        pattern, selector, tiles_here, picked, preferred_element_type=jnp.float32
    )


def shards(
    features,
    tile_vals,
    tile_rows,
    tile_cols,
    tile_count,
    cut_weights,
    send_idx,
    send_count,
    weight,
    bias,
    cotangent,
):
    rows_dev, feature_width = features.shape
    tile_side = tile_vals.shape[1]
    blk_size = lax.axis_size("blk")
    dom_size = lax.axis_size("dom")
    position = lax.axis_index("blk")
    row_blocks = rows_dev // tile_side
    slot_count = tile_vals.shape[0] // blk_size
    send_most = send_idx.shape[1] // dom_size
    tiles = tile_vals.reshape(blk_size, slot_count, tile_side, tile_side)
    row_ids = tile_rows.reshape(blk_size, slot_count)
    col_ids = tile_cols.reshape(blk_size, slot_count)
    counts = tile_count.reshape(blk_size)
    slot_ids = jnp.arange(slot_count, dtype=jnp.int32)
    live_all = slot_ids[None, :] < counts[:, None]
    sent_rows = send_idx.reshape(dom_size * send_most)
    sent_live = (
        jnp.arange(send_most, dtype=jnp.int32)[None, :] < send_count.reshape(dom_size)[:, None]
    )
    outgoing = jnp.take(features, sent_rows, axis=0).reshape(dom_size, send_most, feature_width)
    outgoing = jnp.where(sent_live[:, :, None], outgoing, jnp.zeros_like(outgoing))
    received = lax.all_to_all(outgoing, "dom", split_axis=0, concat_axis=0, tiled=True)
    cut_part = jnp.dot(
        cut_weights,
        received.reshape(dom_size * send_most, feature_width),
        preferred_element_type=jnp.float32,
    )
    empty = jnp.zeros((row_blocks, tile_side, feature_width), jnp.float32)
    piece = lax.all_gather(features, "blk", axis=0, tiled=True)
    start = jnp.int32(0)
    piece_rows = piece.shape[0]
    padded = pad_piece(piece, tile_side)

    def one_step(source_step, partial_value):
        source = (position - source_step) % blk_size
        lowest = source * rows_dev
        touches = (lowest < start + piece_rows) & (lowest + rows_dev > start)

        def work(inner):
            firsts = lowest + col_ids[source_step] * tile_side
            picked, inside = pick_blocks(padded, piece_rows, firsts, tile_side)
            return accumulate(
                inner,
                tiles[source_step],
                picked,
                row_ids[source_step],
                inside & live_all[source_step],
                False,
            )

        return lax.cond(touches, work, lambda inner: inner, partial_value)

    intra = lax.fori_loop(0, blk_size, one_step, empty).reshape(rows_dev, feature_width)
    aggregated = (intra + cut_part).astype(jnp.bfloat16)
    pre = jnp.dot(aggregated, weight, preferred_element_type=jnp.float32) + bias
    sigmoid_pre = jax.nn.sigmoid(pre)
    out_y = (pre * sigmoid_pre).astype(jnp.bfloat16)
    dpre = (cotangent.astype(jnp.float32) * sigmoid_pre * (1.0 + pre * (1.0 - sigmoid_pre))).astype(
        jnp.bfloat16
    )
    weight_term = lax.dot_general(
        aggregated, dpre, (((0,), (0,)), ((), ())), preferred_element_type=jnp.float32
    )
    bias_term = jnp.sum(dpre.astype(jnp.float32), axis=0)
    dz_rows = lax.dot_general(
        dpre, weight, (((1,), (1,)), ((), ())), preferred_element_type=jnp.float32
    ).astype(jnp.bfloat16)
    cut_back = lax.dot_general(
        cut_weights, dz_rows, (((0,), (0,)), ((), ())), preferred_element_type=jnp.float32
    ).astype(jnp.bfloat16)
    returned = lax.all_to_all(
        cut_back.reshape(dom_size, send_most, feature_width),
        "dom",
        split_axis=0,
        concat_axis=0,
        tiled=True,
    )
    returned = jnp.where(sent_live[:, :, None], returned.astype(jnp.float32), 0.0)
    cut_grad = (
        jnp.zeros((rows_dev, feature_width), jnp.float32)
        .at[sent_rows]
        .add(returned.reshape(dom_size * send_most, feature_width))
    )
    dz_blocks = dz_rows.reshape(row_blocks, tile_side, feature_width)
    row_total = rows_dev * lax.axis_size("blk")

    def one_panel(panel_idx):
        source_step = (position - panel_idx) % blk_size
        picked = jnp.take(dz_blocks, row_ids[source_step], axis=0)
        return accumulate(
            empty, tiles[source_step], picked, col_ids[source_step], live_all[source_step], True
        )

    panel_ids = jnp.arange(row_total // rows_dev, dtype=jnp.int32)
    intra_grad = lax.psum_scatter(
        lax.map(one_panel, panel_ids).reshape(row_total, feature_width),
        "blk",
        scatter_dimension=0,
        tiled=True,
    )
    weight_sum, bias_sum = lax.psum((weight_term, bias_term), ("dom", "blk"))
    scale = 1.0 / math.sqrt(dom_size * blk_size * rows_dev)
    grad_x = (intra_grad + cut_grad).astype(jnp.bfloat16)
    return (out_y, grad_x, weight_sum * scale, bias_sum * scale)


def solution(mesh):
    in_specs = (
        P(("dom", "blk"), None),
        P(("dom", "blk"), None, None),
        P(("dom", "blk"), None),
        P(("dom", "blk"), None),
        P(("dom", "blk"), None),
        P(("dom", "blk"), None),
        P(("dom", "blk"), None),
        P(("dom", "blk"), None),
        P(),
        P(),
        P(("dom", "blk"), None),
    )
    out_specs = (P(("dom", "blk"), None), P(("dom", "blk"), None), P(), P())
    return jax.shard_map(shards, mesh=mesh, in_specs=in_specs, out_specs=out_specs, check_vma=False)
```

profile of v0, /device:TPU:0, one launch (start us, length us, event | category | flops | bytes accessed | tf_op | source)
XLA Modules:
  0.0 325.4 jit_solution(1108997307019440022)
XLA Ops:
  7.2 0.7 all-gather.2.cloned.1.call-update
  7.9 0.7 reduce.2
  8.7 0.7 fusion.45
  9.4 2.2 gather_fusion.1
  11.6 0.7 iota_compare_fusion.2
  12.3 0.8 select_select_fusion
  13.1 5.2 %all-to-all-start = ((bf16[8,48,128]{2,1,0:T(8,128)(2,1)}), bf16[8,48,128]{2,1,0:T(8,128)(2,1)S(1)}, u32[]{:S(2)}, u32[]{:S(2)}) async-start(bf16[8,48,128]{2,1,0:T(8,128)(2,1)} %select_select_fusion), calls=%async_computation | async-start | bytes 196608 | tf_op jit(solution)/shard_map/all_to_all | solution.py:66
  18.9 1.3 reduce.10
  20.2 1.3 reduce.9
  21.7 0.7 iota_compare_fusion.3
  22.4 17.8 %all-gather.2.cloned.1.call-done = bf16[4096,128]{1,0:T(8,128)(2,1)} async-done(((bf16[1024,128]{1,0:T(8,128)(2,1)}), bf16[4096,128]{1,0:T(8,128)(2,1)}) %all-gather.2.cloned.1.call-update) | async-done | bytes 1048592 | tf_op jit(solution)/shard_map/all_gather | solution.py:73
  40.3 1.3 pad_maximum_fusion
  41.6 99.8 %while.34 = (s32[]{:T(128)}, f32[8,128,128]{1,0,2:T(8,128)S(1)}, s32[]{:T(128)}, s32[4,18]{1,0:T(4,128)S(1)}, bf16[4352,128]{1,0:T(8,128)(2,1)S(1)}, /*index=5*/...) while((s32[]{:T(128)}, f32[8,128,128]{1,0,2:T(8,128)S(1)}, ...), condition=%wide.region_3.4_spmd.clone, body=%wide.region_0.3_spmd.clone.sunk | while | flops 80347744 | bytes 3475381 | solution.py:97
  41.7 24.9 %conditional.3 = (f32[8,128,128]{1,0,2:T(8,128)S(1)}) conditional(s32[]{:T(128)} %convert_element_type.66, f32[8,128,128]{1,0,2:T(8,128)S(1)} %get-tuple-element.590, (s32[]{:T(128)}, s32[]{:T(128)}, s32[4,18]{1,0:T(4,128)S(1)}, bf16[4352,128]{1,0:T(8,128)(2,1)S(1)}, bf16[4,18,128,128]{3,2,1,0:T(8,128)(2,1)}, /*index=5*/s32[4,18]{1,0:T(4,128)S(1)}, ...), branch_computations={%region_1.1_spmd, %region_2.2_spmd} | conditional | flops 80347728 | bytes 3474709 | solution.py:95
  41.9 22.6 %while.32 = (s32[]{:T(128)}, bf16[4352,128]{1,0:T(8,128)(2,1)S(1)}, s32[18,2]{0,1:T(2,128)S(1)}, bf16[18,128,128]{2,1,0:T(8,128)(2,1)S(1)}, s32[]{:T(128)}) while((s32[]{:T(128)}, bf16[4352,128]{1,0:T(8,128)(2,1)S(1)}, s32[18,2]{0,1:T(2,128)S(1)}, bf16[18,128,128]{2,1,0:T(8,128)(2,1)S(1)}, s32[]{:T(128)}) %tuple.94), condition=%wide.while_cond, body=%wide.while_body.sunk | while | flops 2 | bytes 65641 | solution.py:15
  42.5 0.6 bitcast_dynamic-update-slice_fusion.2
  43.7 0.6 bitcast_dynamic-update-slice_fusion.2
  45.0 0.6 bitcast_dynamic-update-slice_fusion.2
  46.2 0.6 bitcast_dynamic-update-slice_fusion.2
  47.5 0.6 bitcast_dynamic-update-slice_fusion.2
  48.8 0.6 bitcast_dynamic-update-slice_fusion.2
  50.0 0.6 bitcast_dynamic-update-slice_fusion.2
  51.3 0.6 bitcast_dynamic-update-slice_fusion.2
  52.5 0.6 bitcast_dynamic-update-slice_fusion.2
  53.8 0.6 bitcast_dynamic-update-slice_fusion.2
  55.0 0.6 bitcast_dynamic-update-slice_fusion.2
  56.3 0.6 bitcast_dynamic-update-slice_fusion.2
  57.5 0.6 bitcast_dynamic-update-slice_fusion.2
  58.8 0.6 bitcast_dynamic-update-slice_fusion.2
  60.1 0.6 bitcast_dynamic-update-slice_fusion.2
  61.3 0.6 bitcast_dynamic-update-slice_fusion.2
  64.5 1.6 fusion.10
  66.6 24.9 %conditional.3 = (f32[8,128,128]{1,0,2:T(8,128)S(1)}) conditional(s32[]{:T(128)} %convert_element_type.66, f32[8,128,128]{1,0,2:T(8,128)S(1)} %get-tuple-element.590, (s32[]{:T(128)}, s32[]{:T(128)}, s32[4,18]{1,0:T(4,128)S(1)}, bf16[4352,128]{1,0:T(8,128)(2,1)S(1)}, bf16[4,18,128,128]{3,2,1,0:T(8,128)(2,1)}, /*index=5*/s32[4,18]{1,0:T(4,128)S(1)}, ...), branch_computations={%region_1.1_spmd, %region_2.2_spmd} | conditional | flops 80347728 | bytes 3474709 | solution.py:95
  66.8 22.6 %while.32 = (s32[]{:T(128)}, bf16[4352,128]{1,0:T(8,128)(2,1)S(1)}, s32[18,2]{0,1:T(2,128)S(1)}, bf16[18,128,128]{2,1,0:T(8,128)(2,1)S(1)}, s32[]{:T(128)}) while((s32[]{:T(128)}, bf16[4352,128]{1,0:T(8,128)(2,1)S(1)}, s32[18,2]{0,1:T(2,128)S(1)}, bf16[18,128,128]{2,1,0:T(8,128)(2,1)S(1)}, s32[]{:T(128)}) %tuple.94), condition=%wide.while_cond, body=%wide.while_body.sunk | while | flops 2 | bytes 65641 | solution.py:15
  89.4 1.6 fusion.10
  91.6 24.9 %conditional.3 = (f32[8,128,128]{1,0,2:T(8,128)S(1)}) conditional(s32[]{:T(128)} %convert_element_type.66, f32[8,128,128]{1,0,2:T(8,128)S(1)} %get-tuple-element.590, (s32[]{:T(128)}, s32[]{:T(128)}, s32[4,18]{1,0:T(4,128)S(1)}, bf16[4352,128]{1,0:T(8,128)(2,1)S(1)}, bf16[4,18,128,128]{3,2,1,0:T(8,128)(2,1)}, /*index=5*/s32[4,18]{1,0:T(4,128)S(1)}, ...), branch_computations={%region_1.1_spmd, %region_2.2_spmd} | conditional | flops 80347728 | bytes 3474709 | solution.py:95
  91.7 22.6 %while.32 = (s32[]{:T(128)}, bf16[4352,128]{1,0:T(8,128)(2,1)S(1)}, s32[18,2]{0,1:T(2,128)S(1)}, bf16[18,128,128]{2,1,0:T(8,128)(2,1)S(1)}, s32[]{:T(128)}) while((s32[]{:T(128)}, bf16[4352,128]{1,0:T(8,128)(2,1)S(1)}, s32[18,2]{0,1:T(2,128)S(1)}, bf16[18,128,128]{2,1,0:T(8,128)(2,1)S(1)}, s32[]{:T(128)}) %tuple.94), condition=%wide.while_cond, body=%wide.while_body.sunk | while | flops 2 | bytes 65641 | solution.py:15
  114.4 1.6 fusion.10
  116.5 24.9 %conditional.3 = (f32[8,128,128]{1,0,2:T(8,128)S(1)}) conditional(s32[]{:T(128)} %convert_element_type.66, f32[8,128,128]{1,0,2:T(8,128)S(1)} %get-tuple-element.590, (s32[]{:T(128)}, s32[]{:T(128)}, s32[4,18]{1,0:T(4,128)S(1)}, bf16[4352,128]{1,0:T(8,128)(2,1)S(1)}, bf16[4,18,128,128]{3,2,1,0:T(8,128)(2,1)}, /*index=5*/s32[4,18]{1,0:T(4,128)S(1)}, ...), branch_computations={%region_1.1_spmd, %region_2.2_spmd} | conditional | flops 80347728 | bytes 3474709 | solution.py:95
  116.7 22.6 %while.32 = (s32[]{:T(128)}, bf16[4352,128]{1,0:T(8,128)(2,1)S(1)}, s32[18,2]{0,1:T(2,128)S(1)}, bf16[18,128,128]{2,1,0:T(8,128)(2,1)S(1)}, s32[]{:T(128)}) while((s32[]{:T(128)}, bf16[4352,128]{1,0:T(8,128)(2,1)S(1)}, s32[18,2]{0,1:T(2,128)S(1)}, bf16[18,128,128]{2,1,0:T(8,128)(2,1)S(1)}, s32[]{:T(128)}) %tuple.94), condition=%wide.while_cond, body=%wide.while_body.sunk | while | flops 2 | bytes 65641 | solution.py:15
  139.3 1.6 fusion.10
  141.8 2.5 convert_reduce_fusion
  144.4 0.9 fusion.46
  145.6 20.2 %while.33 = (s32[]{:T(128)}, f32[4,8,128,128]{3,2,1,0:T(8,128)}, s32[4]{0:T(128)S(1)}, s32[]{:T(128)}, s32[4,18]{1,0:T(4,128)S(1)}, /*index=5*/bf16[8,128,128]{2...) while((s32[]{:T(128)}, f32[4,8,128,128]{3,2,1,0:T(8,128)}, ...), condition=%wide.region_5.6_spmd, body=%wide.region_4.5_spmd.sunk | while | flops 80512464 | bytes 6165470 | solution.py:140
  147.0 0.7 gather_fusion
  147.7 1.5 fusion.71
  149.8 0.8 constant_dynamic-update-slice_fusion.2
  152.0 0.7 gather_fusion
  152.7 1.5 fusion.71
  154.9 0.9 constant_dynamic-update-slice_fusion.2
  157.1 0.7 gather_fusion
  157.7 1.5 fusion.71
  159.9 0.9 constant_dynamic-update-slice_fusion.2
  162.1 0.7 gather_fusion
  162.8 1.5 fusion.71
  165.0 0.9 constant_dynamic-update-slice_fusion.2
  166.2 0.8 copy.19
  166.9 3.7 %all-to-all-start.1 = ((bf16[8,48,128]{2,1,0:T(8,128)(2,1)}), bf16[8,48,128]{2,1,0:T(8,128)(2,1)S(1)}, u32[]{:S(2)}, u32[]{:S(2)}) async-start(bf16[8,48,128]{2,1,0:T(8,128)(2,1)} %bitcast.26), calls=%async_computation.2 | async-start | bytes 196608 | tf_op jit(solution)/shard_map/all_to_all | solution.py:115
  170.6 40.6 %psum.15 = f32[256]{0:T(256)S(1)} all-reduce(f32[256]{0:T(256)S(1)} %get-tuple-element.426), channel_id=1, replica_groups=mesh['dom'=8,'blk'=4] {'dom','blk'}, use_global_device_ids=true, to_apply=%region_10.11 | all-reduce | flops 256 | bytes 2048 | tf_op jit(solution)/shard_map/psum | solution.py:145
  211.7 56.0 %all-reduce.3.cloned.1.call-done = f32[128,256]{1,0:T(8,128)} async-done(((f32[128,256]{1,0:T(8,128)}), f32[128,256]{1,0:T(8,128)}) %all-reduce.3.cloned.1.call-update) | async-done | bytes 131088 | tf_op jit(solution)/shard_map/psum | solution.py:145
  267.7 1.6 broadcast_multiply_fusion
  269.4 43.5 %reduce-scatter.2.cloned.1.call-done = f32[1024,128]{1,0:T(8,128)} async-done(((f32[4096,128]{1,0:T(8,128)}), f32[1024,128]{1,0:T(8,128)}) %reduce-scatter.2.cloned.1.call-update) | async-done | bytes 524304 | tf_op jit(solution)/shard_map/reduce_scatter | solution.py:139
  312.9 4.2 %scatter_fusion = f32[1024,128]{1,0:T(8,128)} fusion(f32[1024,128]{1,0:T(8,128)} %reduce-scatter.2.cloned.1.call-done, s32[384]{0:T(512)S(1)} %fusion.45, f32[384,128]{1,0:T(8,128)S(1)} %bitcast.102), kind=kCustom, calls=%fused_computation.2 | custom fusion | flops 49152 | bytes 591360 | tf_op jit(solution)/shard_map/scatter-add | solution.py:126
  317.1 1.8 convert_element_type.50
  (293 shorter events, 88.9 us)
Async XLA Ops:
  7.2 134.2 %copy-start = (bf16[1024,384]{1,0:T(8,128)(2,1)S(1)}, bf16[1024,384]{1,0:T(8,128)(2,1)}, u32[]{:S(2)}) copy-start(bf16[1024,384]{1,0:T(8,128)(2,1)} %param.22) | copy-start | bytes 2359300
  7.2 33.1 %all-gather.2.cloned.1.call-start = ((), (), s32[]{:S(2)}) async-start(), calls=%async_computation.3 | async-start | bytes 1310720 | tf_op jit(solution)/shard_map/all_gather | solution.py:73
  7.9 33.7 %copy-start.2 = (s32[1,4]{1,0:T(1,128)S(1)}, s32[1,4]{1,0:T(1,128)}, u32[]{:S(2)}) copy-start(s32[1,4]{1,0:T(1,128)} %param.21) | copy-start | bytes 52
  13.1 128.3 %all-to-all-start = ((bf16[8,48,128]{2,1,0:T(8,128)(2,1)}), bf16[8,48,128]{2,1,0:T(8,128)(2,1)S(1)}, u32[]{:S(2)}, u32[]{:S(2)}) async-start(bf16[8,48,128]{2,1,0:T(8,128)(2,1)} %select_select_fusion), calls=%async_computation | async-start | bytes 196608 | tf_op jit(solution)/shard_map/all_to_all | solution.py:66
  18.3 249.4 %all-reduce.3.cloned.1.call-start = ((), (), s32[]{:S(2)}) async-start(), calls=%async_computation.5 | async-start | bytes 262144 | tf_op jit(solution)/shard_map/psum | solution.py:145
  41.6 100.2 %copy-start.1 = (bf16[128,256]{1,0:T(8,128)(2,1)S(1)}, bf16[128,256]{1,0:T(8,128)(2,1)}, u32[]{:S(2)}) copy-start(bf16[128,256]{1,0:T(8,128)(2,1)} %param.25) | copy-start | bytes 196612
  41.6 100.2 %copy-start.3 = (f32[256]{0:T(256)S(1)}, f32[256]{0:T(256)}, u32[]{:S(2)}) copy-start(f32[256]{0:T(256)} %param.26) | copy-start | bytes 3076
  145.6 167.3 %reduce-scatter.2.cloned.1.call-start = ((), (), s32[]{:S(2)}) async-start(), calls=%async_computation.4 | async-start | bytes 2621440 | tf_op jit(solution)/shard_map/reduce_scatter | solution.py:139
  166.9 102.3 %all-to-all-start.1 = ((bf16[8,48,128]{2,1,0:T(8,128)(2,1)}), bf16[8,48,128]{2,1,0:T(8,128)(2,1)S(1)}, u32[]{:S(2)}, u32[]{:S(2)}) async-start(bf16[8,48,128]{2,1,0:T(8,128)(2,1)} %bitcast.26), calls=%async_computation.2 | async-start | bytes 196608 | tf_op jit(solution)/shard_map/all_to_all | solution.py:115
Sparse Core Ops, SparseCore 0:
  9.6 30.6 all-gather.1
  145.7 121.9 all-reduce.2
  270.0 42.8 reduce-scatter.1
where the time goes:
time: 327 us; the launch traced here: 325 us
  waiting for transfers between devices  118 us (36%)
  local copies, waits for them, and re-layouts  102 us (31%)
  blocking collectives  40.6 us (12%)
  matrix products  20.5 us (6%)
  other arithmetic  16.4 us (5%)
  between operations  13.9 us (4%)
  starting transfers between devices  8.96 us (3%)
  loops' own time  4.92 us (2%)
    gather x216, local copies, waits for them, and re-layouts  89 us
    psum x1, waiting for transfers between devices, shards(): weight_sum, bias_sum = lax.psum((weight_term, bias_term), ('dom', 'blk'))  56 us
    reduce_scatter x1, waiting for transfers between devices, shards(): lax.psum_scatter(lax.map(one_panel, panel_ids).reshape(row_total, feature...  43.5 us
    psum x1, blocking collectives, shards(): weight_sum, bias_sum = lax.psum((weight_term, bias_term), ('dom', 'blk'))  40.6 us
    all_gather x1, waiting for transfers between devices, shards(): piece = lax.all_gather(features, 'blk', axis=0, tiled=True)  17.8 us
    dot_general x16, matrix products, accumulate(): jnp.einsum(pattern, selector, tiles_here, picked, preferred_element_type=...  16 us
  transfers between devices with their start and end apart: 5, of which 3 were waited for; matrix products, arithmetic and copies ran while one was open for 40% of the time, Pallas kernels for 0%

commit v1 on v0

--- a/solution.py
+++ b/solution.py
@@ -142,7 +142,7 @@
         scatter_dimension=0,
         tiled=True,
     )
-    weight_sum, bias_sum = lax.psum((weight_term, bias_term), ("dom", "blk"))
+    weight_sum, bias_sum = lax.psum(lax.psum((weight_term, bias_term), "blk"), "dom")
     scale = 1.0 / math.sqrt(dom_size * blk_size * rows_dev)
     grad_x = (intra_grad + cut_grad).astype(jnp.bfloat16)
     return (out_y, grad_x, weight_sum * scale, bias_sum * scale)

time: 327 us -> 295 us (0.902)
  blocking collectives: 40.6 us -> 22.9 us
  waiting for transfers between devices: 118 us -> 104 us
    psum x1 -> x2, blocking collectives: 40.6 us -> 22.9 us  [the longest x1 12.4 us: shards(): lax.psum(lax.psum((weight_term, bias_term), 'blk'), 'dom')]
    psum x1 -> x2, waiting for transfers between devices: 56 us -> 41.2 us  [the longest x1 33.7 us: shards(): lax.psum((weight_term, bias_term), 'blk')]
  transfers between devices with their start and end apart: 5 -> 6, of which waited for: 3 -> 4; matrix products, arithmetic and copies ran while one was open for 40% -> 44% of each run, Pallas kernels for 0% -> 0%
where the time goes in v1:
time: 295 us; the launch traced here: 293 us
  waiting for transfers between devices  104 us (35%)
  local copies, waits for them, and re-layouts  102 us (35%)
  blocking collectives  22.9 us (8%)
  matrix products  20.5 us (7%)
  other arithmetic  16.4 us (6%)
  between operations  13.9 us (5%)
  starting transfers between devices  8.92 us (3%)
  loops' own time  4.92 us (2%)
    gather x216, local copies, waits for them, and re-layouts  89 us
    reduce_scatter x1, waiting for transfers between devices, shards(): lax.psum_scatter(lax.map(one_panel, panel_ids).reshape(row_total, feature...  43.8 us
    psum x1, waiting for transfers between devices, shards(): lax.psum((weight_term, bias_term), 'blk')  33.7 us
    all_gather x1, waiting for transfers between devices, shards(): piece = lax.all_gather(features, 'blk', axis=0, tiled=True)  17.8 us
    dot_general x16, matrix products, accumulate(): jnp.einsum(pattern, selector, tiles_here, picked, preferred_element_type=...  16 us
    psum x1, blocking collectives, shards(): lax.psum(lax.psum((weight_term, bias_term), 'blk'), 'dom')  12.4 us
    psum x1, blocking collectives, shards(): lax.psum((weight_term, bias_term), 'blk')  10.5 us
    psum x1, waiting for transfers between devices, shards(): lax.psum(lax.psum((weight_term, bias_term), 'blk'), 'dom')  7.46 us
  transfers between devices with their start and end apart: 6, of which 4 were waited for; matrix products, arithmetic and copies ran while one was open for 44% of the time, Pallas kernels for 0%

profile of v1, /device:TPU:0, one launch (start us, length us, event | category | flops | bytes accessed | tf_op | source)
XLA Modules:
  0.0 293.3 jit_solution(17038252428437830140)
XLA Ops:
  7.2 0.7 all-gather.2.cloned.1.call-update
  7.9 0.7 reduce.2
  8.7 0.7 fusion.45
  9.4 2.2 gather_fusion.1
  11.6 0.7 iota_compare_fusion.2
  12.3 0.8 select_select_fusion
  13.1 5.2 %all-to-all-start = ((bf16[8,48,128]{2,1,0:T(8,128)(2,1)}), bf16[8,48,128]{2,1,0:T(8,128)(2,1)S(1)}, u32[]{:S(2)}, u32[]{:S(2)}) async-start(bf16[8,48,128]{2,1,0:T(8,128)(2,1)} %select_select_fusion), calls=%async_computation | async-start | bytes 196608 | tf_op jit(solution)/shard_map/all_to_all | solution.py:66
  18.9 1.3 reduce.10
  20.2 1.3 reduce.9
  21.7 0.7 iota_compare_fusion.3
  22.4 17.8 %all-gather.2.cloned.1.call-done = bf16[4096,128]{1,0:T(8,128)(2,1)} async-done(((bf16[1024,128]{1,0:T(8,128)(2,1)}), bf16[4096,128]{1,0:T(8,128)(2,1)}) %all-gather.2.cloned.1.call-update) | async-done | bytes 1048592 | tf_op jit(solution)/shard_map/all_gather | solution.py:73
  40.3 1.3 pad_maximum_fusion
  41.6 99.8 %while.34 = (s32[]{:T(128)}, f32[8,128,128]{1,0,2:T(8,128)S(1)}, s32[]{:T(128)}, s32[4,18]{1,0:T(4,128)S(1)}, bf16[4352,128]{1,0:T(8,128)(2,1)S(1)}, /*index=5*/...) while((s32[]{:T(128)}, f32[8,128,128]{1,0,2:T(8,128)S(1)}, ...), condition=%wide.region_3.4_spmd.clone, body=%wide.region_0.3_spmd.clone.sunk | while | flops 80347744 | bytes 3475381 | solution.py:97
  41.7 24.9 %conditional.3 = (f32[8,128,128]{1,0,2:T(8,128)S(1)}) conditional(s32[]{:T(128)} %convert_element_type.66, f32[8,128,128]{1,0,2:T(8,128)S(1)} %get-tuple-element.590, (s32[]{:T(128)}, s32[]{:T(128)}, s32[4,18]{1,0:T(4,128)S(1)}, bf16[4352,128]{1,0:T(8,128)(2,1)S(1)}, bf16[4,18,128,128]{3,2,1,0:T(8,128)(2,1)}, /*index=5*/s32[4,18]{1,0:T(4,128)S(1)}, ...), branch_computations={%region_1.1_spmd, %region_2.2_spmd} | conditional | flops 80347728 | bytes 3474709 | solution.py:95
  41.9 22.6 %while.32 = (s32[]{:T(128)}, bf16[4352,128]{1,0:T(8,128)(2,1)S(1)}, s32[18,2]{0,1:T(2,128)S(1)}, bf16[18,128,128]{2,1,0:T(8,128)(2,1)S(1)}, s32[]{:T(128)}) while((s32[]{:T(128)}, bf16[4352,128]{1,0:T(8,128)(2,1)S(1)}, s32[18,2]{0,1:T(2,128)S(1)}, bf16[18,128,128]{2,1,0:T(8,128)(2,1)S(1)}, s32[]{:T(128)}) %tuple.94), condition=%wide.while_cond, body=%wide.while_body.sunk | while | flops 2 | bytes 65641 | solution.py:15
  42.5 0.6 bitcast_dynamic-update-slice_fusion.2
  43.7 0.6 bitcast_dynamic-update-slice_fusion.2
  45.0 0.6 bitcast_dynamic-update-slice_fusion.2
  46.2 0.6 bitcast_dynamic-update-slice_fusion.2
  47.5 0.6 bitcast_dynamic-update-slice_fusion.2
  48.8 0.6 bitcast_dynamic-update-slice_fusion.2
  50.0 0.6 bitcast_dynamic-update-slice_fusion.2
  51.3 0.6 bitcast_dynamic-update-slice_fusion.2
  52.5 0.6 bitcast_dynamic-update-slice_fusion.2
  53.8 0.6 bitcast_dynamic-update-slice_fusion.2
  55.0 0.6 bitcast_dynamic-update-slice_fusion.2
  56.3 0.6 bitcast_dynamic-update-slice_fusion.2
  57.6 0.6 bitcast_dynamic-update-slice_fusion.2
  58.8 0.6 bitcast_dynamic-update-slice_fusion.2
  64.5 1.6 fusion.10
  66.6 24.9 %conditional.3 = (f32[8,128,128]{1,0,2:T(8,128)S(1)}) conditional(s32[]{:T(128)} %convert_element_type.66, f32[8,128,128]{1,0,2:T(8,128)S(1)} %get-tuple-element.590, (s32[]{:T(128)}, s32[]{:T(128)}, s32[4,18]{1,0:T(4,128)S(1)}, bf16[4352,128]{1,0:T(8,128)(2,1)S(1)}, bf16[4,18,128,128]{3,2,1,0:T(8,128)(2,1)}, /*index=5*/s32[4,18]{1,0:T(4,128)S(1)}, ...), branch_computations={%region_1.1_spmd, %region_2.2_spmd} | conditional | flops 80347728 | bytes 3474709 | solution.py:95
  66.8 22.6 %while.32 = (s32[]{:T(128)}, bf16[4352,128]{1,0:T(8,128)(2,1)S(1)}, s32[18,2]{0,1:T(2,128)S(1)}, bf16[18,128,128]{2,1,0:T(8,128)(2,1)S(1)}, s32[]{:T(128)}) while((s32[]{:T(128)}, bf16[4352,128]{1,0:T(8,128)(2,1)S(1)}, s32[18,2]{0,1:T(2,128)S(1)}, bf16[18,128,128]{2,1,0:T(8,128)(2,1)S(1)}, s32[]{:T(128)}) %tuple.94), condition=%wide.while_cond, body=%wide.while_body.sunk | while | flops 2 | bytes 65641 | solution.py:15
  89.4 1.6 fusion.10
  91.6 24.9 %conditional.3 = (f32[8,128,128]{1,0,2:T(8,128)S(1)}) conditional(s32[]{:T(128)} %convert_element_type.66, f32[8,128,128]{1,0,2:T(8,128)S(1)} %get-tuple-element.590, (s32[]{:T(128)}, s32[]{:T(128)}, s32[4,18]{1,0:T(4,128)S(1)}, bf16[4352,128]{1,0:T(8,128)(2,1)S(1)}, bf16[4,18,128,128]{3,2,1,0:T(8,128)(2,1)}, /*index=5*/s32[4,18]{1,0:T(4,128)S(1)}, ...), branch_computations={%region_1.1_spmd, %region_2.2_spmd} | conditional | flops 80347728 | bytes 3474709 | solution.py:95
  91.7 22.6 %while.32 = (s32[]{:T(128)}, bf16[4352,128]{1,0:T(8,128)(2,1)S(1)}, s32[18,2]{0,1:T(2,128)S(1)}, bf16[18,128,128]{2,1,0:T(8,128)(2,1)S(1)}, s32[]{:T(128)}) while((s32[]{:T(128)}, bf16[4352,128]{1,0:T(8,128)(2,1)S(1)}, s32[18,2]{0,1:T(2,128)S(1)}, bf16[18,128,128]{2,1,0:T(8,128)(2,1)S(1)}, s32[]{:T(128)}) %tuple.94), condition=%wide.while_cond, body=%wide.while_body.sunk | while | flops 2 | bytes 65641 | solution.py:15
  114.4 1.6 fusion.10
  116.5 24.9 %conditional.3 = (f32[8,128,128]{1,0,2:T(8,128)S(1)}) conditional(s32[]{:T(128)} %convert_element_type.66, f32[8,128,128]{1,0,2:T(8,128)S(1)} %get-tuple-element.590, (s32[]{:T(128)}, s32[]{:T(128)}, s32[4,18]{1,0:T(4,128)S(1)}, bf16[4352,128]{1,0:T(8,128)(2,1)S(1)}, bf16[4,18,128,128]{3,2,1,0:T(8,128)(2,1)}, /*index=5*/s32[4,18]{1,0:T(4,128)S(1)}, ...), branch_computations={%region_1.1_spmd, %region_2.2_spmd} | conditional | flops 80347728 | bytes 3474709 | solution.py:95
  116.7 22.6 %while.32 = (s32[]{:T(128)}, bf16[4352,128]{1,0:T(8,128)(2,1)S(1)}, s32[18,2]{0,1:T(2,128)S(1)}, bf16[18,128,128]{2,1,0:T(8,128)(2,1)S(1)}, s32[]{:T(128)}) while((s32[]{:T(128)}, bf16[4352,128]{1,0:T(8,128)(2,1)S(1)}, s32[18,2]{0,1:T(2,128)S(1)}, bf16[18,128,128]{2,1,0:T(8,128)(2,1)S(1)}, s32[]{:T(128)}) %tuple.94), condition=%wide.while_cond, body=%wide.while_body.sunk | while | flops 2 | bytes 65641 | solution.py:15
  139.3 1.6 fusion.10
  141.8 2.5 convert_reduce_fusion
  144.4 0.9 fusion.46
  145.6 33.7 %all-reduce.4.cloned.1.call-done = f32[128,256]{1,0:T(8,128)} async-done(((f32[128,256]{1,0:T(8,128)}), f32[128,256]{1,0:T(8,128)}) %all-reduce.4.cloned.1.call-update) | async-done | bytes 131088 | tf_op jit(solution)/shard_map/psum | solution.py:145
  179.5 20.2 %while.33 = (s32[]{:T(128)}, f32[4,8,128,128]{3,2,1,0:T(8,128)}, s32[4]{0:T(128)S(1)}, s32[]{:T(128)}, s32[4,18]{1,0:T(4,128)S(1)}, /*index=5*/bf16[8,128,128]{2...) while((s32[]{:T(128)}, f32[4,8,128,128]{3,2,1,0:T(8,128)}, ...), condition=%wide.region_5.6_spmd, body=%wide.region_4.5_spmd.sunk | while | flops 80512464 | bytes 6165470 | solution.py:140
  180.8 0.7 gather_fusion
  181.5 1.5 fusion.71
  183.7 0.8 constant_dynamic-update-slice_fusion.2
  185.8 0.7 gather_fusion
  186.5 1.5 fusion.71
  188.7 0.9 constant_dynamic-update-slice_fusion.2
  190.9 0.7 gather_fusion
  191.5 1.5 fusion.71
  193.7 0.9 constant_dynamic-update-slice_fusion.2
  195.9 0.7 gather_fusion
  196.6 1.5 fusion.71
  198.8 0.9 constant_dynamic-update-slice_fusion.2
  200.0 0.8 copy.19
  200.7 3.6 %all-to-all-start.1 = ((bf16[8,48,128]{2,1,0:T(8,128)(2,1)}), bf16[8,48,128]{2,1,0:T(8,128)(2,1)S(1)}, u32[]{:S(2)}, u32[]{:S(2)}) async-start(bf16[8,48,128]{2,1,0:T(8,128)(2,1)} %bitcast.26), calls=%async_computation.2 | async-start | bytes 196608 | tf_op jit(solution)/shard_map/all_to_all | solution.py:115
  204.3 10.5 %psum.30 = f32[256]{0:T(256)S(1)} all-reduce(f32[256]{0:T(256)S(1)} %get-tuple-element.426), channel_id=1, replica_groups=mesh['dom'=8,'blk'=4] {'blk'}, use_global_device_ids=true, to_apply=%region_11.12 | all-reduce | flops 256 | bytes 2048 | tf_op jit(solution)/shard_map/psum | solution.py:145
  214.8 12.4 %psum.31 = f32[256]{0:T(256)S(1)} all-reduce(f32[256]{0:T(256)S(1)} %psum.30), channel_id=1, replica_groups=mesh['dom'=8,'blk'=4] {'dom'}, use_global_device_ids=true, to_apply=%region_12.13 | all-reduce | flops 256 | bytes 2048 | tf_op jit(solution)/shard_map/psum | solution.py:145
  227.9 7.5 %all-reduce.6.cloned.1.call-done = f32[128,256]{1,0:T(8,128)} async-done(((f32[128,256]{1,0:T(8,128)}), f32[128,256]{1,0:T(8,128)}) %all-reduce.6.cloned.1.call-update) | async-done | bytes 131088 | tf_op jit(solution)/shard_map/psum | solution.py:145
  235.4 1.6 broadcast_multiply_fusion
  236.9 43.8 %reduce-scatter.2.cloned.1.call-done = f32[1024,128]{1,0:T(8,128)} async-done(((f32[4096,128]{1,0:T(8,128)}), f32[1024,128]{1,0:T(8,128)}) %reduce-scatter.2.cloned.1.call-update) | async-done | bytes 524304 | tf_op jit(solution)/shard_map/reduce_scatter | solution.py:139
  280.8 4.2 %scatter_fusion = f32[1024,128]{1,0:T(8,128)} fusion(f32[1024,128]{1,0:T(8,128)} %reduce-scatter.2.cloned.1.call-done, s32[384]{0:T(512)S(1)} %fusion.45, f32[384,128]{1,0:T(8,128)S(1)} %bitcast.102), kind=kCustom, calls=%fused_computation.2 | custom fusion | flops 49152 | bytes 591360 | tf_op jit(solution)/shard_map/scatter-add | solution.py:126
  285.0 1.8 convert_element_type.50
  (297 shorter events, 90.2 us)
Async XLA Ops:
  7.2 134.2 %copy-start = (bf16[1024,384]{1,0:T(8,128)(2,1)S(1)}, bf16[1024,384]{1,0:T(8,128)(2,1)}, u32[]{:S(2)}) copy-start(bf16[1024,384]{1,0:T(8,128)(2,1)} %param.22) | copy-start | bytes 2359300
  7.2 33.1 %all-gather.2.cloned.1.call-start = ((), (), s32[]{:S(2)}) async-start(), calls=%async_computation.3 | async-start | bytes 1310720 | tf_op jit(solution)/shard_map/all_gather | solution.py:73
  7.9 33.7 %copy-start.2 = (s32[1,4]{1,0:T(1,128)S(1)}, s32[1,4]{1,0:T(1,128)}, u32[]{:S(2)}) copy-start(s32[1,4]{1,0:T(1,128)} %param.21) | copy-start | bytes 52
  13.1 128.3 %all-to-all-start = ((bf16[8,48,128]{2,1,0:T(8,128)(2,1)}), bf16[8,48,128]{2,1,0:T(8,128)(2,1)S(1)}, u32[]{:S(2)}, u32[]{:S(2)}) async-start(bf16[8,48,128]{2,1,0:T(8,128)(2,1)} %select_select_fusion), calls=%async_computation | async-start | bytes 196608 | tf_op jit(solution)/shard_map/all_to_all | solution.py:66
  18.3 161.1 %all-reduce.4.cloned.1.call-start = ((), (), s32[]{:S(2)}) async-start(), calls=%async_computation.5 | async-start | bytes 262144 | tf_op jit(solution)/shard_map/psum | solution.py:145
  41.6 100.2 %copy-start.1 = (bf16[128,256]{1,0:T(8,128)(2,1)S(1)}, bf16[128,256]{1,0:T(8,128)(2,1)}, u32[]{:S(2)}) copy-start(bf16[128,256]{1,0:T(8,128)(2,1)} %param.25) | copy-start | bytes 196612
  41.6 100.2 %copy-start.3 = (f32[256]{0:T(256)S(1)}, f32[256]{0:T(256)}, u32[]{:S(2)}) copy-start(f32[256]{0:T(256)} %param.26) | copy-start | bytes 3076
  145.3 90.1 %all-reduce.6.cloned.1.call-start = ((), (), s32[]{:S(2)}) async-start(), calls=%async_computation.6 | async-start | bytes 262144 | tf_op jit(solution)/shard_map/psum | solution.py:145
  179.4 101.4 %reduce-scatter.2.cloned.1.call-start = ((), (), s32[]{:S(2)}) async-start(), calls=%async_computation.4 | async-start | bytes 2621440 | tf_op jit(solution)/shard_map/reduce_scatter | solution.py:139
  200.7 27.0 %all-to-all-start.1 = ((bf16[8,48,128]{2,1,0:T(8,128)(2,1)}), bf16[8,48,128]{2,1,0:T(8,128)(2,1)S(1)}, u32[]{:S(2)}, u32[]{:S(2)}) async-start(bf16[8,48,128]{2,1,0:T(8,128)(2,1)} %bitcast.26), calls=%async_computation.2 | async-start | bytes 196608 | tf_op jit(solution)/shard_map/all_to_all | solution.py:115
Sparse Core Ops, SparseCore 0:
  9.6 30.6 all-gather.1
  145.4 33.9 all-reduce.3
  182.7 52.6 all-reduce.5
  237.5 43.2 reduce-scatter.1
